TPU v7x, 128 devices: a whole 4x4x4 slice. The times are simulated.
128 devices in a mesh: dp: 16 (over x, y), proto: 8 (over z, core).
Axes of the slice: x: 4, y: 4, z: 4, core: 2. Of those that a mesh axis runs over, the one named last changes fastest.
Arguments:
- teacher_feat: bfloat16 [16384, 256], P('dp'), may hold values from -80 to 80
- student_feat: bfloat16 [16384, 256], P('dp'), may hold values from -80 to 80
- proto_weight: bfloat16 [256, 65536], P('dp', 'proto'), may hold values from -60 to 60
Outputs:
- weight_grad: float32 [256, 65536], P('dp', 'proto')
- loss: float32 [], replicated
All inputs are finite; a program needn't handle non-finite values.
Results may differ from a plain program's by a relative error of at most 0.0004.
Values may be sent and summed in bfloat16 or wider, within the bound.
A program may use at most 192 MiB of HBM per device.

v0:
```python
import jax
import jax.numpy as jnp
from jax import lax
from jax.sharding import PartitionSpec as P

ITERS = 3


EPS = 1e-06
TEACHER_TEMP = 0.07
STUDENT_TEMP = 0.1


def unit_rows(feat):
    values = feat.astype(jnp.float32)
    scaled = values / jnp.sqrt(jnp.sum(values * values, axis=1, keepdims=True) + EPS)
    return scaled.astype(jnp.bfloat16)


def body(teacher_feat, student_feat, proto_weight):
    t_hat = unit_rows(teacher_feat)
    s_hat = unit_rows(student_feat)
    total_rows = teacher_feat.shape[0] * lax.axis_size("dp")
    total_cols = proto_weight.shape[1] * lax.axis_size("proto")
    whole = lax.all_gather(proto_weight, "dp", axis=0, tiled=True)
    norms = jnp.sqrt(jnp.sum(jnp.square(whole.astype(jnp.float32)), axis=0) + EPS)
    cos_t = jnp.dot(t_hat, whole, preferred_element_type=jnp.float32) / norms
    cos_s = jnp.dot(s_hat, whole, preferred_element_type=jnp.float32) / norms
    targets = jnp.exp(cos_t / TEACHER_TEMP)
    for step in range(ITERS):
        mass = lax.psum(jnp.sum(targets, axis=0), "dp")
        targets = targets / (mass * total_cols)
        if step < ITERS - 1:
            row_mass = lax.psum(jnp.sum(targets, axis=1), "proto")
            targets = targets / (row_mass[:, None] * total_rows)
    logits = cos_s / STUDENT_TEMP
    expo = jnp.exp(logits)
    row_mass = lax.psum(jnp.sum(targets, axis=1), "proto")
    soft_total = lax.psum(jnp.sum(expo, axis=1), "proto")
    targets = targets / (row_mass[:, None] * total_rows) * total_rows
    log_total = jnp.log(soft_total)
    probs = expo / soft_total[:, None]
    local_loss = jnp.sum(targets * (log_total[:, None] - logits))
    loss = lax.psum(local_loss, ("dp", "proto")) / total_rows
    grad_cos = ((probs - targets) / (total_rows * STUDENT_TEMP)).astype(jnp.bfloat16)
    col_part = jnp.sum(cos_s * grad_cos.astype(jnp.float32), axis=0)
    own_rows = proto_weight.shape[0]
    full_grad = jnp.einsum("bd,bk->dk", s_hat, grad_cos, preferred_element_type=jnp.float32)
    summed, col_sum = lax.psum((full_grad, col_part), "dp")
    first_row = lax.axis_index("dp") * own_rows
    grad_rows = lax.dynamic_slice_in_dim(summed, first_row, own_rows, 0)
    own_dirs = proto_weight.astype(jnp.float32) / norms
    weight_grad = (grad_rows - own_dirs * col_sum) / norms
    return (weight_grad, loss)


def solution(mesh):
    in_specs = (P("dp", None), P("dp", None), P("dp", "proto"))
    out_specs = (P("dp", "proto"), P())
    return jax.shard_map(body, mesh=mesh, in_specs=in_specs, out_specs=out_specs, check_vma=False)
```

profile of v0, /device:TPU:0, one launch (start us, length us, event | category | flops | bytes accessed | tf_op | source)
XLA Modules:
  0.0 610.5 jit_solution(12703899980585300396)
XLA Ops:
  7.2 0.7 all-gather.2.cloned.1.call-update
  7.9 0.0 all-reduce.3.cloned.1.call-start
  7.9 1.3 fusion.14
  9.2 1.3 fusion.12
  10.5 53.5 %all-gather.2.cloned.1.call-done = bf16[256,8192]{1,0:T(8,128)(2,1)} async-done(((bf16[16,8192]{1,0:T(8,128)(2,1)}), bf16[256,8192]{1,0:T(8,128)(2,1)}) %all-gather.2.cloned.1.call-update) | async-done | bytes 4194320 | tf_op jit(solution)/shard_map/all_gather | solution.py:25
  64.0 3.1 multiply_reduce_fusion.2
  67.1 16.9 %fusion.21 = (f32[8192]{0:T(1024)S(1)}, f32[1024,8192]{1,0:T(8,128)}) fusion(f32[8192]{0:T(1024)S(1)} %add_sqrt_fusion, bf16[256,8192]{1,0:T(8,128)(2,1)} %all-gather.2.cloned.1.call-done, bf16[1024,256]{1,0:T(8,128)(2,1)} %param.3, f32[1024]{0:T(1024)S(1)} %add_sqrt_fusion.1), kind=kOutput, calls=%fused_computation.42 | convolution fusion | flops 4320911360 | bytes 38342656 | tf_op jit(solution)/shard_map/dot_general | solution.py:27
  84.1 72.4 %psum.71 = f32[8192]{0:T(1024)S(1)} all-reduce(f32[8192]{0:T(1024)S(1)} %get-tuple-element.9), channel_id=1, replica_groups=mesh['dp'=16,'proto'=8] {'dp'}, use_global_device_ids=true, to_apply=%region_6.0 | all-reduce | flops 8192 | bytes 65536 | tf_op jit(solution)/shard_map/psum | solution.py:31
  156.4 12.2 %divide_reduce_fusion = f32[1024]{0:T(1024)S(1)} fusion(f32[1024,8192]{1,0:T(8,128)} %get-tuple-element.10, f32[8192]{0:T(1024)S(1)} %broadcast_multiply_fusion.2), kind=kLoop, calls=%fused_computation.14 | loop fusion | flops 16776192 | bytes 33591296 | tf_op jit(solution)/shard_map/reduce_sum | solution.py:34
  168.6 12.4 %psum.72 = f32[1024]{0:T(1024)S(1)} all-reduce(f32[1024]{0:T(1024)S(1)} %divide_reduce_fusion), channel_id=1, replica_groups=mesh['dp'=16,'proto'=8] {'proto'}, use_global_device_ids=true, to_apply=%region_8.0 | all-reduce | flops 1024 | bytes 8192 | tf_op jit(solution)/shard_map/psum | solution.py:34
  181.1 14.1 %fusion.8 = f32[8192]{0:T(1024)S(1)} fusion(f32[1024,8192]{1,0:T(8,128)} %get-tuple-element.10, f32[1024]{0:T(1024)S(1)} %broadcast_multiply_fusion.5, f32[8192]{0:T(1024)S(1)} %broadcast_multiply_fusion.2), kind=kLoop, calls=%fused_computation.15 | loop fusion | flops 25157632 | bytes 33624064 | tf_op jit(solution)/shard_map/reduce_sum | solution.py:31
  195.1 69.5 %psum.73 = f32[8192]{0:T(1024)S(1)} all-reduce(f32[8192]{0:T(1024)S(1)} %fusion.8), channel_id=1, replica_groups=mesh['dp'=16,'proto'=8] {'dp'}, use_global_device_ids=true, to_apply=%region_10.0 | all-reduce | flops 8192 | bytes 65536 | tf_op jit(solution)/shard_map/psum | solution.py:31
  264.7 14.1 %fusion.9 = f32[1024]{0:T(1024)S(1)} fusion(f32[1024,8192]{1,0:T(8,128)} %get-tuple-element.10, f32[8192]{0:T(1024)S(1)} %broadcast_multiply_fusion.1, f32[1024]{0:T(1024)S(1)} %broadcast_multiply_fusion.5, f32[8192]{0:T(1024)S(1)} %broadcast_multiply_fusion.2), kind=kLoop, calls=%fused_computation.16 | loop fusion | flops 33553408 | bytes 33628160 | tf_op jit(solution)/shard_map/reduce_sum | solution.py:34
  278.8 12.4 %psum.74 = f32[1024]{0:T(1024)S(1)} all-reduce(f32[1024]{0:T(1024)S(1)} %fusion.9), channel_id=1, replica_groups=mesh['dp'=16,'proto'=8] {'proto'}, use_global_device_ids=true, to_apply=%region_12.0 | all-reduce | flops 1024 | bytes 8192 | tf_op jit(solution)/shard_map/psum | solution.py:34
  291.3 14.5 %fusion.10 = f32[8192]{0:T(1024)S(1)} fusion(f32[1024,8192]{1,0:T(8,128)} %get-tuple-element.10, f32[1024]{0:T(1024)S(1)} %broadcast_multiply_fusion.4, f32[8192]{0:T(1024)S(1)} %broadcast_multiply_fusion.1, f32[1024]{0:T(1024)S(1)} %broadcast_multiply_fusion.5, f32[8192]{0:T(1024)S(1)} %broadcast_multiply_fusion.2), kind=kLoop, calls=%fused_computation.17 | loop fusion | flops 41934848 | bytes 33660928 | tf_op jit(solution)/shard_map/reduce_sum | solution.py:31
  305.8 69.7 %psum.75 = f32[8192]{0:T(1024)S(1)} all-reduce(f32[8192]{0:T(1024)S(1)} %fusion.10), channel_id=1, replica_groups=mesh['dp'=16,'proto'=8] {'dp'}, use_global_device_ids=true, to_apply=%region_14.0 | all-reduce | flops 8192 | bytes 65536 | tf_op jit(solution)/shard_map/psum | solution.py:31
  375.5 15.4 %fusion.11 = f32[1024]{0:T(1024)S(1)} fusion(f32[1024,8192]{1,0:T(8,128)} %get-tuple-element.10, f32[8192]{0:T(1024)S(1)} %broadcast_multiply_fusion, f32[1024]{0:T(1024)S(1)} %broadcast_multiply_fusion.4, f32[8192]{0:T(1024)S(1)} %broadcast_multiply_fusion.1, f32[1024]{0:T(1024)S(1)} %broadcast_multiply_fusion.5, f32[8192]{0:T(1024)S(1)} %broadcast_multiply_fusion.2), kind=kLoop, calls=%fused_computation.18 | loop fusion | flops 50330624 | bytes 33665024 | tf_op jit(solution)/shard_map/reduce_sum | solution.py:38
  391.0 13.4 %exponential_reduce_fusion = (f32[1024]{0:T(1024)S(1)}, f32[1024,8192]{1,0:T(8,128)}) fusion(f32[8192]{0:T(1024)S(1)} %add_sqrt_fusion, bf16[256,8192]{1,0:T(8,128)(2,1)S(1)} %copy-done, bf16[1024,256]{1,0:T(8,128)(2,1)S(1)} %copy-done.1, f32[1024]{0:T(1024)S(1)} %add_sqrt_fusion.2), kind=kOutput, calls=%fused_computation.19 | convolution fusion | flops 4320918528 | bytes 38313984 | tf_op jit(solution)/shard_map/dot_general | solution.py:28
  404.4 12.6 %all-reduce = (f32[1024]{0:T(1024)S(1)}, f32[1024]{0:T(1024)S(1)}) all-reduce(f32[1024]{0:T(1024)S(1)} %get-tuple-element.7, f32[1024]{0:T(1024)S(1)} %fusion.11), channel_id=1, replica_groups=mesh['dp'=16,'proto'=8] {'proto'}, use_global_device_ids=true, to_apply=%region_3.0 | all-reduce | flops 2048 | bytes 16384 | tf_op jit(solution)/shard_map/psum | solution.py:39
  417.1 32.4 %multiply_reduce_fusion = (f32[]{:T(128)}, f32[8192]{0:T(1024)S(1)}, bf16[1024,8192]{1,0:T(8,128)(2,1)}) fusion(f32[1024,8192]{1,0:T(8,128)} %get-tuple-element.8, f32[1024]{0:T(1024)S(1)} %log.3, f32[1024,8192]{1,0:T(8,128)} %get-tuple-element.10, f32[1024]{0:T(1024)S(1)} %broadcast_multiply_fusion.3, f32[8192]{0:T(1024)S(1)} %broadcast_multiply_fusion, ...), kind=kLoop, calls=%fused_computation.10 | loop fusion | flops 150986752 | bytes 84037632 | tf_op jit(solution)/shard_map/reduce_sum | solution.py:43
  449.4 12.9 %fusion.18 = f32[256,8192]{1,0:T(8,128)} fusion(bf16[1024,8192]{1,0:T(8,128)(2,1)} %get-tuple-element.6, bf16[1024,256]{1,0:T(8,128)(2,1)S(1)} %copy-done.1, f32[1024]{0:T(1024)S(1)} %add_sqrt_fusion.2), kind=kOutput, calls=%fused_computation.41 | convolution fusion | flops 4295753728 | bytes 25694208 | tf_op jit(solution)/shard_map/bd,bk->dk/dot_general | solution.py:48
  462.4 64.5 %psum.79 = f32[]{:T(128)} all-reduce(f32[]{:T(128)} %get-tuple-element.2), channel_id=1, replica_groups=mesh['dp'=16,'proto'=8] {'dp','proto'}, use_global_device_ids=true, to_apply=%region_21.0 | all-reduce | flops 1 | bytes 8 | tf_op jit(solution)/shard_map/psum | solution.py:44
  527.6 73.0 %psum.78 = f32[8192]{0:T(1024)S(1)} all-reduce(f32[8192]{0:T(1024)S(1)} %get-tuple-element.3), channel_id=1, replica_groups=mesh['dp'=16,'proto'=8] {'dp'}, use_global_device_ids=true, to_apply=%region_19.0 | all-reduce | flops 8192 | bytes 65536 | tf_op jit(solution)/shard_map/psum | solution.py:49
  600.6 1.9 subtract_divide_fusion
  (19 shorter events, 0.1 us)
Async XLA Ops:
  7.2 56.9 %all-gather.2.cloned.1.call-start = ((), (), s32[]{:S(2)}) async-start(), calls=%async_computation | async-start | bytes 4456448 | tf_op jit(solution)/shard_map/all_gather | solution.py:25
  7.9 592.7 %all-reduce.3.cloned.1.call-start = ((), (), s32[]{:S(2)}) async-start(), calls=%async_computation.1 | async-start | bytes 16777216 | tf_op jit(solution)/shard_map/psum | solution.py:49
  291.3 99.7 %copy-start.1 = (bf16[1024,256]{1,0:T(8,128)(2,1)S(1)}, bf16[1024,256]{1,0:T(8,128)(2,1)}, u32[]{:S(2)}) copy-start(bf16[1024,256]{1,0:T(8,128)(2,1)} %param.4) | copy-start | bytes 1572868
  375.5 15.4 %copy-start = (bf16[256,8192]{1,0:T(8,128)(2,1)S(1)}, bf16[256,8192]{1,0:T(8,128)(2,1)}, u32[]{:S(2)}) copy-start(bf16[256,8192]{1,0:T(8,128)(2,1)} %all-gather.2.cloned.1.call-done) | copy-start | bytes 12582916
  449.4 151.1 %copy-start.2 = (bf16[16,8192]{1,0:T(8,128)(2,1)S(1)}, bf16[16,8192]{1,0:T(8,128)(2,1)}, u32[]{:S(2)}) copy-start(bf16[16,8192]{1,0:T(8,128)(2,1)} %param.5) | copy-start | bytes 786436
Sparse Core Ops, SparseCore 0:
  10.1 53.8 all-gather.1
  462.5 136.4 all-reduce.2
where the time goes:
time: 611 us; the launch traced here: 610 us
  blocking collectives  387 us (63%)
  other arithmetic  110 us (18%)
  waiting for transfers between devices  54.2 us (9%)
  matrix products  43.3 us (7%)
  between operations  15.9 us (3%)
    psum x3, blocking collectives, body(): mass = lax.psum(jnp.sum(targets, axis=0), 'dp')  212 us
    psum x1, blocking collectives, body(): summed, col_sum = lax.psum((full_grad, col_part), 'dp')  73 us
    psum x1, blocking collectives, body(): loss = lax.psum(local_loss, ('dp', 'proto')) / total_rows  64.5 us
    all_gather x1, waiting for transfers between devices, body(): whole = lax.all_gather(proto_weight, 'dp', axis=0, tiled=True)  53.5 us
    reduce_sum x3, other arithmetic, body(): row_mass = lax.psum(jnp.sum(targets, axis=1), 'proto')  41.7 us
    reduce_sum x1, other arithmetic, body(): local_loss = jnp.sum(targets * (log_total[:, None] - logits))  32.4 us
    reduce_sum x2, other arithmetic, body(): mass = lax.psum(jnp.sum(targets, axis=0), 'dp')  28.6 us
    psum x2, blocking collectives, body(): row_mass = lax.psum(jnp.sum(targets, axis=1), 'proto')  24.9 us
  transfers between devices with their start and end apart: 2, of which 1 were waited for; matrix products, arithmetic and copies ran while one was open for 0% of the time, Pallas kernels for 0%

commit v1 on v0

v1 whole, which is shorter than its diff:
```python
import functools
import math

import jax
import jax.numpy as jnp
from jax import lax
from jax.experimental import pallas as pl
from jax.experimental.pallas import tpu as pltpu
from jax.sharding import PartitionSpec as P

ITERS = 3
EPS = 1e-06
TEACHER_TEMP = 0.07
STUDENT_TEMP = 0.1
LOG2E = math.log2(math.e)
LANES = 128
MESH = pl.DeviceIdType.MESH
F32 = jnp.float32
BF16 = jnp.bfloat16

W_A2A, T_GATHER, S_GATHER = 0, 1, 2
COL = (3, 4, 5)
ROW = (6, 7, 8)
OUT_A2A, LOSS_PROTO, LOSS_DP = 9, 10, 11
W_PLUS, W_MINUS, W_HALF_A, W_HALF_B = 12, 13, 14, 15
W_CORE = 16
G_CORE = 20
G_HALF_A, G_HALF_B, G_PLUS, G_MINUS = 24, 25, 26, 27
STAGES = 28


def unit_rows(feat):
    values = feat.astype(F32)
    scaled = values / jnp.sqrt(jnp.sum(values * values, axis=1, keepdims=True) + EPS)
    return scaled.astype(BF16)


def fold_rows(x):
    n, c = x.shape
    return jnp.sum(x.reshape(n // 8, 8, c), axis=0)


def fold_lanes(x):
    total = x[:, :LANES]
    for j in range(1, x.shape[1] // LANES):
        total = total + x[:, j * LANES:(j + 1) * LANES]
    return total


def kernel(
    nd, np_, tile,
    teacher, student, weight,
    out, loss_out,
    t_raw, s_raw, t_all, s_all, s_t, w_all, e_ref,
    at_ref, as_ref, inv_ref, v_ref, rb_ref, sb_ref, racc, sacc,
    colx, rowx, g_tile, g_send, g_recv, g_own, half_a, half_b, g_z, out_recv,
    loss_p, loss_d,
    ssem, rsem, lsem,
):
    d = lax.axis_index("dp")
    p = lax.axis_index("proto")
    nz = np_ // 2
    partner = p + 1 - 2 * lax.rem(p, 2)
    plus = lax.rem(p + 2, np_)
    minus = lax.rem(p + np_ - 2, np_)
    chunk = t_raw.shape[0]
    rows = t_all.shape[0]
    depth, cols = w_all.shape[1:]
    own_depth = depth // nd
    ntiles = rows // tile
    total_rows = rows * np_
    total_cols = cols * np_ * nd

    def other(block):
        return block + 1 - 2 * lax.rem(block, 2)

    def remote(src, dst, stage, **where):
        return pltpu.make_async_remote_copy(
            src_ref=src, dst_ref=dst, send_sem=ssem.at[stage], recv_sem=rsem.at[stage],
            device_id=where, device_id_type=MESH)

    def to_all(axis, me, n, make):
        def step(o, carry):
            make(lax.rem(me + o, n), axis).start()
            return carry
        lax.fori_loop(1, n, step, 0)

    def wait_bytes(sem, ref):
        pltpu.make_async_copy(ref, ref, sem).wait()

    barrier = pltpu.get_barrier_semaphore()

    def greet(axis, me, n):
        def step(o, carry):
            pl.semaphore_signal(barrier, inc=1, device_id={axis: lax.rem(me + o, n)}, device_id_type=MESH)
            return carry
        lax.fori_loop(1, n, step, 0)

    greet("dp", d, nd)
    greet("proto", p, np_)

    load_t = pltpu.make_async_copy(teacher.at[pl.ds(p * chunk, chunk)], t_raw, lsem.at[0])
    load_s = pltpu.make_async_copy(student.at[pl.ds(p * chunk, chunk)], s_raw, lsem.at[1])
    own_rows = pl.ds(d * own_depth, own_depth)
    load_w = pltpu.make_async_copy(
        weight.at[:, pl.ds(d * cols, cols)], w_all.at[p, own_rows], lsem.at[2])
    load_t.start()
    load_s.start()
    load_w.start()
    load_t.wait()
    own_chunk = pl.ds(d * chunk, chunk)
    t_all[own_chunk, :] = unit_rows(t_raw[...])
    pl.semaphore_wait(barrier, nd + np_ - 2)

    to_all("dp", d, nd, lambda j, axis: remote(
        weight.at[:, pl.ds(j * cols, cols)], w_all.at[p, own_rows], W_A2A, **{axis: j}))
    to_all("dp", d, nd, lambda j, axis: remote(
        t_all.at[own_chunk], t_all.at[own_chunk], T_GATHER, **{axis: j}))
    load_s.wait()
    s_all[own_chunk, :] = unit_rows(s_raw[...])

    load_w.wait()
    wait_bytes(rsem.at[W_A2A], w_all.at[p, pl.ds(0, depth - own_depth)])
    half = depth // 2
    top, bottom = pl.ds(0, half), pl.ds(half, half)
    copies = []

    def go(copy):
        copy.start()
        copies.append(copy)
        return copy

    opposite = lax.rem(p + 4, np_)
    up = go(remote(w_all.at[p], w_all.at[p], W_PLUS, proto=plus))
    down = go(remote(w_all.at[p], w_all.at[p], W_MINUS, proto=minus))
    core = [None] * 4
    core[0] = go(remote(w_all.at[p], w_all.at[p], W_CORE, proto=partner))
    to_all("dp", d, nd, lambda j, axis: remote(
        s_all.at[own_chunk], s_all.at[own_chunk], S_GATHER, **{axis: j}))
    up.wait_recv()
    pass_a = go(remote(w_all.at[minus, top], w_all.at[minus, top], W_HALF_A, proto=plus))
    core[1] = go(remote(w_all.at[minus], w_all.at[minus], W_CORE + 1, proto=partner))
    down.wait_recv()
    pass_b = go(remote(w_all.at[plus, bottom], w_all.at[plus, bottom], W_HALF_B, proto=minus))
    core[2] = go(remote(w_all.at[plus], w_all.at[plus], W_CORE + 2, proto=partner))

    wait_bytes(rsem.at[T_GATHER], t_all.at[pl.ds(0, rows - chunk)])

    def first_pass(block):
        w = w_all[block].astype(F32)
        inv = 1.0 / jnp.sqrt(jnp.sum(w * w, axis=0, keepdims=True) + EPS)
        inv_ref[block] = inv
        at_ref[block] = inv * (LOG2E / TEACHER_TEMP)
        as_ref[block] = inv * (LOG2E / STUDENT_TEMP)

        def step(i, acc):
            part = pl.ds(i * tile, tile)
            dots = jnp.dot(t_all[part, :], w_all[block], preferred_element_type=F32)
            e = jnp.exp2(dots * at_ref[block])
            e_ref[block, part, :] = e
            return acc + fold_rows(e)

        acc = lax.fori_loop(0, ntiles, step, jnp.zeros((8, cols), F32))
        colx[0, p, block] = jnp.sum(acc, axis=0, keepdims=True)

    first_pass(p)
    core[0].wait_recv()
    first_pass(partner)
    first_pass(minus)
    first_pass(plus)
    core[1].wait_recv()
    first_pass(other(minus))
    core[2].wait_recv()
    first_pass(other(plus))
    pass_a.wait_recv()
    pass_b.wait_recv()
    core[3] = go(remote(w_all.at[opposite], w_all.at[opposite], W_CORE + 3, proto=partner))
    first_pass(opposite)
    core[3].wait_recv()
    first_pass(other(opposite))

    def send_cols(it):
        to_all("proto", p, np_, lambda j, axis: remote(
            colx.at[it, p], colx.at[it, p], COL[it], **{axis: j}))

    def take_cols(it):
        wait_bytes(rsem.at[COL[it]], colx.at[it, pl.ds(0, np_ - 1)])
        mass = colx[it, 0]
        for j in range(1, np_):
            mass = mass + colx[it, j]
        v_ref[...] = 1.0 / (mass * total_cols)

    def dense(acc_ref):
        lines = [
            jnp.sum(acc_ref[c * LANES:(c + 1) * LANES, :].T, axis=0, keepdims=True)
            for c in range(rows // LANES)]
        return jnp.concatenate(lines, axis=0)

    def spread(x, ref):
        for c in range(rows // LANES):
            ref[c * LANES:(c + 1) * LANES, :] = jnp.broadcast_to(x[c:c + 1, :], (LANES, LANES)).T

    def send_rows(it):
        def make(j, axis):
            if it < ITERS - 1:
                return remote(rowx.at[it, d, 0], rowx.at[it, d, 0], ROW[it], **{axis: j})
            return remote(rowx.at[it, d], rowx.at[it, d], ROW[it], **{axis: j})
        to_all("dp", d, nd, make)

    def row_total(it, kind):
        total = rowx[it, 0, kind]
        for j in range(1, nd):
            total = total + rowx[it, j, kind]
        return total

    def take_rows(it):
        if it < ITERS - 1:
            wait_bytes(rsem.at[ROW[it]], rowx.at[it, pl.ds(0, nd - 1), 0])
        else:
            wait_bytes(rsem.at[ROW[it]], rowx.at[it, pl.ds(0, nd - 1)])
        return 1.0 / (row_total(it, 0) * total_rows)

    lane_chunks = cols // LANES

    def row_pass(it):
        span = 64

        def step(i, carry):
            part = pl.ds(i * span, span)
            acc = None
            for b in range(np_):
                for j in range(lane_chunks):
                    lanes = slice(j * LANES, (j + 1) * LANES)
                    term = e_ref[b, part, lanes] * v_ref[b, :, lanes]
                    acc = term if acc is None else acc + term
            racc[part, :] = acc
            return carry

        lax.fori_loop(0, rows // span, step, 0)
        rowx[it, d, 0] = dense(racc)

    def col_pass(it):
        pair = 2

        def step(b2, carry):
            def inner(i, accs):
                accs = list(accs)
                for g in range(8):
                    part = pl.ds(i * 64 + g * 8, 8)
                    r = rb_ref[part, :]
                    for k in range(pair):
                        for j in range(lane_chunks):
                            n = k * lane_chunks + j
                            accs[n] = accs[n] + e_ref[b2 * pair + k, part, j * LANES:(j + 1) * LANES] * r
                return tuple(accs)

            zero = jnp.zeros((8, LANES), F32)
            accs = lax.fori_loop(0, rows // 64, inner, (zero,) * (pair * lane_chunks))
            for k in range(pair):
                for j in range(lane_chunks):
                    colx[it, p, b2 * pair + k, :, j * LANES:(j + 1) * LANES] = jnp.sum(
                        accs[k * lane_chunks + j], axis=0, keepdims=True)
            return carry

        lax.fori_loop(0, np_ // pair, step, 0)

    def student_pass(block, first):
        def step(i, carry):
            part = pl.ds(i * tile, tile)
            dots = jnp.dot(s_all[part, :], w_all[block], preferred_element_type=F32)
            sums = fold_lanes(jnp.exp2(dots * as_ref[block]))
            if first:
                sacc[part, :] = sums
            else:
                sacc[part, :] += sums
            return carry
        lax.fori_loop(0, ntiles, step, 0)

    send_cols(0)
    wait_bytes(rsem.at[S_GATHER], s_all.at[pl.ds(0, rows - chunk)])
    for c in range(rows // LANES):
        s_t[:, c * LANES:(c + 1) * LANES] = s_all[c * LANES:(c + 1) * LANES, :].T
    student_pass(0, True)
    student_pass(1, False)
    take_cols(0)
    row_pass(0)
    send_rows(0)
    student_pass(2, False)
    student_pass(3, False)
    spread(take_rows(0), rb_ref)
    col_pass(1)
    send_cols(1)
    student_pass(4, False)
    student_pass(5, False)
    take_cols(1)
    row_pass(1)
    send_rows(1)
    student_pass(6, False)
    student_pass(7, False)
    rowx[2, d, 1] = dense(sacc)
    spread(take_rows(1), rb_ref)
    col_pass(2)
    send_cols(2)
    take_cols(2)
    row_pass(2)
    send_rows(2)
    row_scale = take_rows(2)
    spread(row_scale * (1.0 / STUDENT_TEMP), rb_ref)
    soft_total = row_total(2, 1)
    spread(1.0 / (soft_total * (total_rows * STUDENT_TEMP)), sb_ref)
    lse = jnp.log(soft_total)

    def last_pass(block, dst, acc0):
        def step(i, acc):
            part = pl.ds(i * tile, tile)
            zb = jnp.dot(s_all[part, :], w_all[block], preferred_element_type=F32) * as_ref[block]
            es = jnp.exp2(zb)
            q_scale = rb_ref[part, :]
            p_scale = sb_ref[part, :]
            new = acc
            for j in range(lane_chunks):
                lanes = slice(j * LANES, (j + 1) * LANES)
                q = e_ref[block, part, lanes] * v_ref[block, :, lanes] * q_scale
                g_tile[part, lanes] = (es[:, lanes] * p_scale - q).astype(BF16)
                new = new + fold_rows(q * zb[:, lanes])
            return new

        acc = lax.fori_loop(0, ntiles, step, acc0)
        dst[...] = jnp.dot(s_t[...], g_tile[...], preferred_element_type=F32)
        return acc

    loss_acc = jnp.zeros((8, LANES), F32)
    owners = [opposite, plus, minus, p]
    gsends = [None] * 4
    left, right = slice(0, cols // 2), slice(cols // 2, cols)

    for n in range(4):
        own = owners[n]
        loss_acc = last_pass(other(own), g_send.at[n], loss_acc)
        gsends[n] = go(remote(g_send.at[n], g_recv.at[n], G_CORE + n, proto=partner))
        loss_acc = last_pass(own, g_own.at[n], loss_acc)
        gsends[n].wait_recv()
        if n == 0:
            g_own[0] += g_recv[0]
            ha = go(remote(g_own.at[0, top], half_a, G_HALF_A, proto=plus))
            hb = go(remote(g_own.at[0, bottom], half_b, G_HALF_B, proto=minus))
        elif n == 1:
            g_own[1, bottom] += g_recv[1, bottom]
            ha.wait_recv()
            g_own[1, top] = g_own[1, top] + g_recv[1, top] + half_a[...]
            gp = go(remote(g_own.at[1], g_z.at[0], G_PLUS, proto=plus))
        elif n == 2:
            g_own[2, top] += g_recv[2, top]
            hb.wait_recv()
            g_own[2, bottom] = g_own[2, bottom] + g_recv[2, bottom] + half_b[...]
            gm = go(remote(g_own.at[2], g_z.at[1], G_MINUS, proto=minus))

    first_line = lax.broadcasted_iota(jnp.int32, (8, LANES), 0) == 0
    lse_sum = jnp.broadcast_to(jnp.sum(lse, axis=0, keepdims=True) * (1.0 / nd), (8, LANES))
    loss_scale = total_rows * STUDENT_TEMP / LOG2E
    loss_p[p] = jnp.where(first_line, lse_sum, 0.0) - loss_acc * loss_scale
    to_all("proto", p, np_, lambda j, axis: remote(
        loss_p.at[p], loss_p.at[p], LOSS_PROTO, **{axis: j}))

    gp.wait_recv()
    gm.wait_recv()
    grad = g_own[3] + g_recv[3] + g_z[0] + g_z[1]
    inv = inv_ref[p]
    dirs = w_all[p].astype(F32) * inv
    col = jnp.sum(dirs * grad, axis=0, keepdims=True)
    g_own[3] = (grad - dirs * col) * inv
    to_all("dp", d, nd, lambda j, axis: remote(
        g_own.at[3, pl.ds(j * own_depth, own_depth)], out_recv.at[d], OUT_A2A, **{axis: j}))
    out_recv[d] = g_own[3, own_rows]

    wait_bytes(rsem.at[LOSS_PROTO], loss_p.at[pl.ds(0, np_ - 1)])
    part = loss_p[0]
    for j in range(1, np_):
        part = part + loss_p[j]
    loss_d[d] = part
    to_all("dp", d, nd, lambda j, axis: remote(
        loss_d.at[d], loss_d.at[d], LOSS_DP, **{axis: j}))
    wait_bytes(rsem.at[LOSS_DP], loss_d.at[pl.ds(0, nd - 1)])
    whole = loss_d[0]
    for j in range(1, nd):
        whole = whole + loss_d[j]
    loss_out[...] = jnp.broadcast_to(
        jnp.sum(jnp.sum(whole, axis=0, keepdims=True), axis=1, keepdims=True) * (1.0 / total_rows), (8, LANES))

    wait_bytes(rsem.at[OUT_A2A], out_recv.at[pl.ds(0, nd - 1)])
    for j in range(nd):
        out[:, j * cols:(j + 1) * cols] = out_recv[j]

    for copy in copies:
        copy.wait_send()
    wait_bytes(ssem.at[W_A2A], w_all.at[0, pl.ds(0, depth - own_depth)])
    wait_bytes(ssem.at[T_GATHER], t_all.at[pl.ds(0, rows - chunk)])
    wait_bytes(ssem.at[S_GATHER], s_all.at[pl.ds(0, rows - chunk)])
    for it in range(ITERS):
        wait_bytes(ssem.at[COL[it]], colx.at[it, pl.ds(0, np_ - 1)])
        if it < ITERS - 1:
            wait_bytes(ssem.at[ROW[it]], rowx.at[it, pl.ds(0, nd - 1), 0])
        else:
            wait_bytes(ssem.at[ROW[it]], rowx.at[it, pl.ds(0, nd - 1)])
    wait_bytes(ssem.at[OUT_A2A], out_recv.at[pl.ds(0, nd - 1)])
    wait_bytes(ssem.at[LOSS_PROTO], loss_p.at[pl.ds(0, np_ - 1)])
    wait_bytes(ssem.at[LOSS_DP], loss_d.at[pl.ds(0, nd - 1)])


def body(nd, np_, teacher_feat, student_feat, proto_weight):
    block_rows, depth = teacher_feat.shape
    own_depth, block_cols = proto_weight.shape
    chunk, cols = block_rows // np_, block_cols // nd
    rows = chunk * nd
    tile = min(256, rows)
    vmem = pltpu.VMEM
    out, loss = pl.pallas_call(
        functools.partial(kernel, nd, np_, tile),
        out_shape=(
            jax.ShapeDtypeStruct((own_depth, block_cols), F32),
            jax.ShapeDtypeStruct((8, LANES), F32),
        ),
        in_specs=[pl.BlockSpec(memory_space=pl.ANY)] * 3,
        out_specs=[pl.BlockSpec(memory_space=vmem)] * 2,
        scratch_shapes=[
            vmem((chunk, depth), BF16),
            vmem((chunk, depth), BF16),
            vmem((rows, depth), BF16),
            vmem((rows, depth), BF16),
            vmem((depth, rows), BF16),
            vmem((np_, depth, cols), BF16),
            vmem((np_, rows, cols), F32),
            vmem((np_, 1, cols), F32),
            vmem((np_, 1, cols), F32),
            vmem((np_, 1, cols), F32),
            vmem((np_, 1, cols), F32),
            vmem((rows, LANES), F32),
            vmem((rows, LANES), F32),
            vmem((rows, LANES), F32),
            vmem((rows, LANES), F32),
            vmem((ITERS, np_, np_, 1, cols), F32),
            vmem((ITERS, nd, 2, rows // LANES, LANES), F32),
            vmem((rows, cols), BF16),
            vmem((4, depth, cols), F32),
            vmem((4, depth, cols), F32),
            vmem((4, depth, cols), F32),
            vmem((depth // 2, cols), F32),
            vmem((depth // 2, cols), F32),
            vmem((2, depth, cols), F32),
            vmem((nd, own_depth, cols), F32),
            vmem((np_, 8, LANES), F32),
            vmem((nd, 8, LANES), F32),
            pltpu.SemaphoreType.DMA((STAGES,)),
            pltpu.SemaphoreType.DMA((STAGES,)),
            pltpu.SemaphoreType.DMA((3,)),
        ],
        compiler_params=pltpu.CompilerParams(
            collective_id=0, has_side_effects=True, vmem_limit_bytes=62 * 1024 * 1024),
        cost_estimate=pl.CostEstimate(
            flops=6 * rows * cols * np_ * depth, bytes_accessed=2 ** 21,
            transcendentals=2 * rows * cols * np_),
    )(teacher_feat, student_feat, proto_weight)
    return out, loss[0, 0]


def solution(mesh):
    nd, np_ = mesh.shape["dp"], mesh.shape["proto"]
    in_specs = (P("dp", None), P("dp", None), P("dp", "proto"))
    out_specs = (P("dp", "proto"), P())
    return jax.shard_map(
        functools.partial(body, nd, np_), mesh=mesh, in_specs=in_specs, out_specs=out_specs, check_vma=False)
```

time: 611 us -> 147 us (0.24)
  blocking collectives: 387 us -> 0 us
  Pallas kernels: 0 us -> 143 us
  other arithmetic: 110 us -> 0 us
  waiting for transfers between devices: 54.2 us -> 0 us
  matrix products: 43.3 us -> 0 us
  between operations: 15.9 us -> 0.64 us
    psum x8 -> x0, blocking collectives: 387 us -> none  [the longest x3 212 us: body(): mass = lax.psum(jnp.sum(targets, axis=0), 'dp')]
    pallas_call x0 -> x1, Pallas kernels: none -> 143 us  [body(): pl.pallas_call(functools.partial(kernel, nd, np_, tile), out_shape=(jax.S...]
    reduce_sum x9 -> x0, other arithmetic: 108 us -> none  [the longest x3 41.7 us: body(): row_mass = lax.psum(jnp.sum(targets, axis=1), 'proto')]
    all_gather x1 -> x0, waiting for transfers between devices: 53.5 us -> none  [body(): whole = lax.all_gather(proto_weight, 'dp', axis=0, tiled=True)]
    dot_general x3 -> x0, matrix products: 43.3 us -> none  [the longest x1 16.9 us: body(): cos_t = jnp.dot(t_hat, whole, preferred_element_type=jnp.float32) / norms]
  transfers between devices with their start and end apart: 2 -> 0, of which waited for: 1 -> 0; matrix products, arithmetic and copies ran while one was open for 0% -> 0% of each run, Pallas kernels for 0% -> 0%
where the time goes in v1:
time: 147 us
  Pallas kernels  143 us (97%)
  local copies, waits for them, and re-layouts  3.05 us (2%)
    pallas_call x1, Pallas kernels, body(): pl.pallas_call(functools.partial(kernel, nd, np_, tile), out_shape=(jax.S...  143 us

profile of v1, /device:TPU:0, one launch (start us, length us, event | category | flops | bytes accessed | tf_op | source)
XLA Modules:
  0.0 146.8 jit_solution(2515191184585971290)
XLA Ops:
  0.6 143.2 %shard_map.50 = (f32[16,8192]{1,0:T(8,128)}, f32[8,128]{1,0:T(8,128)}) custom-call(bf16[1024,256]{1,0:T(8,128)(2,1)} %teacher.1, bf16[1024,256]{1,0:T(8,128)(2,1)} %student.1, bf16[16,8192]{1,0:T(8,128)(2,1)} %weight.1), custom_call_target="tpu_custom_call" | custom-call | flops 12884901888 | bytes 2097152 | tf_op jit(solution)/shard_map/pallas_call | solution.py:417
  143.8 1.2 slice.3
  145.0 1.9 %copy.6 = f32[16,8192]{1,0:T(8,128)} copy(f32[16,8192]{1,0:T(8,128)} %get-tuple-element.8) | data formatting | bytes 1048576

commit v2 on v1

--- a/solution.py
+++ b/solution.py
@@ -21,12 +21,14 @@
 W_A2A, T_GATHER, S_GATHER = 0, 1, 2
 COL = (3, 4, 5)
 ROW = (6, 7, 8)
-OUT_A2A, LOSS_PROTO, LOSS_DP = 9, 10, 11
+LOSS_PROTO, LOSS_DP = 10, 11
 W_PLUS, W_MINUS, W_HALF_A, W_HALF_B = 12, 13, 14, 15
 W_CORE = 16
 G_CORE = 20
-G_HALF_A, G_HALF_B, G_PLUS, G_MINUS = 24, 25, 26, 27
-STAGES = 28
+G_HALF_A, G_HALF_B = 28, 29
+G_PLUS, G_MINUS = 30, 32
+OUT_A2A = 34
+STAGES = 36
 
 
 def unit_rows(feat):
@@ -53,7 +55,7 @@
     out, loss_out,
     t_raw, s_raw, t_all, s_all, s_t, w_all, e_ref,
     at_ref, as_ref, inv_ref, v_ref, rb_ref, sb_ref, racc, sacc,
-    colx, rowx, g_tile, g_send, g_recv, g_own, half_a, half_b, g_z, out_recv,
+    colx, rowx, g_tiles, g_send, g_recv, g_own, half_a, half_b, g_z, out_recv,
     loss_p, loss_d,
     ssem, rsem, lsem,
 ):
@@ -114,8 +116,6 @@
 
     to_all("dp", d, nd, lambda j, axis: remote(
         weight.at[:, pl.ds(j * cols, cols)], w_all.at[p, own_rows], W_A2A, **{axis: j}))
-    to_all("dp", d, nd, lambda j, axis: remote(
-        t_all.at[own_chunk], t_all.at[own_chunk], T_GATHER, **{axis: j}))
     load_s.wait()
     s_all[own_chunk, :] = unit_rows(s_raw[...])
 
@@ -136,7 +136,7 @@
     core = [None] * 4
     core[0] = go(remote(w_all.at[p], w_all.at[p], W_CORE, proto=partner))
     to_all("dp", d, nd, lambda j, axis: remote(
-        s_all.at[own_chunk], s_all.at[own_chunk], S_GATHER, **{axis: j}))
+        t_all.at[own_chunk], t_all.at[own_chunk], T_GATHER, **{axis: j}))
     up.wait_recv()
     pass_a = go(remote(w_all.at[minus, top], w_all.at[minus, top], W_HALF_A, proto=plus))
     core[1] = go(remote(w_all.at[minus], w_all.at[minus], W_CORE + 1, proto=partner))
@@ -145,6 +145,8 @@
     core[2] = go(remote(w_all.at[plus], w_all.at[plus], W_CORE + 2, proto=partner))
 
     wait_bytes(rsem.at[T_GATHER], t_all.at[pl.ds(0, rows - chunk)])
+    to_all("dp", d, nd, lambda j, axis: remote(
+        s_all.at[own_chunk], s_all.at[own_chunk], S_GATHER, **{axis: j}))
 
     def first_pass(block):
         w = w_all[block].astype(F32)
@@ -153,14 +155,13 @@
         at_ref[block] = inv * (LOG2E / TEACHER_TEMP)
         as_ref[block] = inv * (LOG2E / STUDENT_TEMP)
 
-        def step(i, acc):
-            part = pl.ds(i * tile, tile)
+        acc = jnp.zeros((8, cols), F32)
+        for i in range(ntiles):
+            part = slice(i * tile, (i + 1) * tile)
             dots = jnp.dot(t_all[part, :], w_all[block], preferred_element_type=F32)
             e = jnp.exp2(dots * at_ref[block])
             e_ref[block, part, :] = e
-            return acc + fold_rows(e)
-
-        acc = lax.fori_loop(0, ntiles, step, jnp.zeros((8, cols), F32))
+            acc = acc + fold_rows(e)
         colx[0, p, block] = jnp.sum(acc, axis=0, keepdims=True)
 
     first_pass(p)
@@ -264,39 +265,34 @@
 
         lax.fori_loop(0, np_ // pair, step, 0)
 
-    def student_pass(block, first):
-        def step(i, carry):
-            part = pl.ds(i * tile, tile)
-            dots = jnp.dot(s_all[part, :], w_all[block], preferred_element_type=F32)
-            sums = fold_lanes(jnp.exp2(dots * as_ref[block]))
-            if first:
-                sacc[part, :] = sums
-            else:
+    def student_pass(first, last):
+        def step(block, carry):
+            for i in range(ntiles):
+                part = slice(i * tile, (i + 1) * tile)
+                dots = jnp.dot(s_all[part, :], w_all[block], preferred_element_type=F32)
+                sums = fold_lanes(jnp.exp2(dots * as_ref[block]))
                 sacc[part, :] += sums
             return carry
-        lax.fori_loop(0, ntiles, step, 0)
+        lax.fori_loop(first, last, step, 0)
 
     send_cols(0)
     wait_bytes(rsem.at[S_GATHER], s_all.at[pl.ds(0, rows - chunk)])
     for c in range(rows // LANES):
         s_t[:, c * LANES:(c + 1) * LANES] = s_all[c * LANES:(c + 1) * LANES, :].T
-    student_pass(0, True)
-    student_pass(1, False)
+    sacc[...] = jnp.zeros_like(sacc)
+    student_pass(0, 2)
     take_cols(0)
     row_pass(0)
     send_rows(0)
-    student_pass(2, False)
-    student_pass(3, False)
+    student_pass(2, 4)
     spread(take_rows(0), rb_ref)
     col_pass(1)
     send_cols(1)
-    student_pass(4, False)
-    student_pass(5, False)
+    student_pass(4, 6)
     take_cols(1)
     row_pass(1)
     send_rows(1)
-    student_pass(6, False)
-    student_pass(7, False)
+    student_pass(6, 8)
     rowx[2, d, 1] = dense(sacc)
     spread(take_rows(1), rb_ref)
     col_pass(2)
@@ -310,50 +306,75 @@
     spread(1.0 / (soft_total * (total_rows * STUDENT_TEMP)), sb_ref)
     lse = jnp.log(soft_total)
 
-    def last_pass(block, dst, acc0):
-        def step(i, acc):
-            part = pl.ds(i * tile, tile)
-            zb = jnp.dot(s_all[part, :], w_all[block], preferred_element_type=F32) * as_ref[block]
+    half_cols = cols // 2
+
+    def unit(block, side, g_tile, acc):
+        base = side * half_cols
+        columns = slice(base, base + half_cols)
+        for i in range(ntiles):
+            part = slice(i * tile, (i + 1) * tile)
+            zb = jnp.dot(s_all[part, :], w_all[block, :, columns],
+                         preferred_element_type=F32) * as_ref[block, :, columns]
             es = jnp.exp2(zb)
             q_scale = rb_ref[part, :]
             p_scale = sb_ref[part, :]
-            new = acc
-            for j in range(lane_chunks):
+            for j in range(half_cols // LANES):
                 lanes = slice(j * LANES, (j + 1) * LANES)
-                q = e_ref[block, part, lanes] * v_ref[block, :, lanes] * q_scale
+                here = slice(base + j * LANES, base + (j + 1) * LANES)
+                q = e_ref[block, part, here] * v_ref[block, :, here] * q_scale
                 g_tile[part, lanes] = (es[:, lanes] * p_scale - q).astype(BF16)
-                new = new + fold_rows(q * zb[:, lanes])
-            return new
-
-        acc = lax.fori_loop(0, ntiles, step, acc0)
-        dst[...] = jnp.dot(s_t[...], g_tile[...], preferred_element_type=F32)
+                acc = acc + fold_rows(q * zb[:, lanes])
         return acc
 
+    owners = [opposite, plus, minus, p]
+    z_copies = {}
+    core_copies = {}
+
+    def chip_sum(n, side):
+        core_copies[n, side].wait_recv()
+        if (n, side) == (1, 0):
+            z_copies["a"].wait_recv()
+            g_own[n, side] = g_own[n, side] + g_recv[n, side] + half_a[...]
+        elif (n, side) == (2, 1):
+            z_copies["b"].wait_recv()
+            g_own[n, side] = g_own[n, side] + g_recv[n, side] + half_b[...]
+        else:
+            g_own[n, side] += g_recv[n, side]
+        mine = g_own.at[n, side]
+        if (n, side) == (0, 0):
+            z_copies["a"] = go(remote(mine, half_a, G_HALF_A, proto=plus))
+        elif (n, side) == (0, 1):
+            z_copies["b"] = go(remote(mine, half_b, G_HALF_B, proto=minus))
+        elif n == 1:
+            z_copies[0, side] = go(remote(mine, g_z.at[0, side], G_PLUS + side, proto=plus))
+        elif n == 2:
+            z_copies[1, side] = go(remote(mine, g_z.at[1, side], G_MINUS + side, proto=minus))
+
+    def gradient(n, side, is_own, g_tile):
+        dst = g_own if is_own else g_send
+        dst[n, side] = jnp.dot(s_t[...], g_tile[...], preferred_element_type=F32)
+
+    order = [(0, 0), (0, 1), (1, 1), (2, 0), (3, 0), (3, 1), (1, 0), (2, 1)]
+    units = [(n, side, is_own) for n, side in order for is_own in (False, True)]
     loss_acc = jnp.zeros((8, LANES), F32)
-    owners = [opposite, plus, minus, p]
-    gsends = [None] * 4
-    left, right = slice(0, cols // 2), slice(cols // 2, cols)
-
-    for n in range(4):
-        own = owners[n]
-        loss_acc = last_pass(other(own), g_send.at[n], loss_acc)
-        gsends[n] = go(remote(g_send.at[n], g_recv.at[n], G_CORE + n, proto=partner))
-        loss_acc = last_pass(own, g_own.at[n], loss_acc)
-        gsends[n].wait_recv()
-        if n == 0:
-            g_own[0] += g_recv[0]
-            ha = go(remote(g_own.at[0, top], half_a, G_HALF_A, proto=plus))
-            hb = go(remote(g_own.at[0, bottom], half_b, G_HALF_B, proto=minus))
-        elif n == 1:
-            g_own[1, bottom] += g_recv[1, bottom]
-            ha.wait_recv()
-            g_own[1, top] = g_own[1, top] + g_recv[1, top] + half_a[...]
-            gp = go(remote(g_own.at[1], g_z.at[0], G_PLUS, proto=plus))
-        elif n == 2:
-            g_own[2, top] += g_recv[2, top]
-            hb.wait_recv()
-            g_own[2, bottom] = g_own[2, bottom] + g_recv[2, bottom] + half_b[...]
-            gm = go(remote(g_own.at[2], g_z.at[1], G_MINUS, proto=minus))
+    waiting = None
+    for k in range(len(units) + 2):
+        if 0 < k <= len(units):
+            gradient(*units[k - 1], g_tiles.at[(k - 1) % 2])
+        if k < len(units):
+            n, side, is_own = units[k]
+            block = owners[n] if is_own else other(owners[n])
+            loss_acc = unit(block, side, g_tiles.at[k % 2], loss_acc)
+        if waiting is not None:
+            chip_sum(*waiting)
+            waiting = None
+        if 0 < k <= len(units):
+            n, side, is_own = units[k - 1]
+            if is_own:
+                waiting = (n, side)
+            else:
+                core_copies[n, side] = go(remote(
+                    g_send.at[n, side], g_recv.at[n, side], G_CORE + 2 * n + side, proto=partner))
 
     first_line = lax.broadcasted_iota(jnp.int32, (8, LANES), 0) == 0
     lse_sum = jnp.broadcast_to(jnp.sum(lse, axis=0, keepdims=True) * (1.0 / nd), (8, LANES))
@@ -361,18 +382,6 @@
     loss_p[p] = jnp.where(first_line, lse_sum, 0.0) - loss_acc * loss_scale
     to_all("proto", p, np_, lambda j, axis: remote(
         loss_p.at[p], loss_p.at[p], LOSS_PROTO, **{axis: j}))
-
-    gp.wait_recv()
-    gm.wait_recv()
-    grad = g_own[3] + g_recv[3] + g_z[0] + g_z[1]
-    inv = inv_ref[p]
-    dirs = w_all[p].astype(F32) * inv
-    col = jnp.sum(dirs * grad, axis=0, keepdims=True)
-    g_own[3] = (grad - dirs * col) * inv
-    to_all("dp", d, nd, lambda j, axis: remote(
-        g_own.at[3, pl.ds(j * own_depth, own_depth)], out_recv.at[d], OUT_A2A, **{axis: j}))
-    out_recv[d] = g_own[3, own_rows]
-
     wait_bytes(rsem.at[LOSS_PROTO], loss_p.at[pl.ds(0, np_ - 1)])
     part = loss_p[0]
     for j in range(1, np_):
@@ -380,6 +389,21 @@
     loss_d[d] = part
     to_all("dp", d, nd, lambda j, axis: remote(
         loss_d.at[d], loss_d.at[d], LOSS_DP, **{axis: j}))
+
+    for side in (0, 1):
+        columns = slice(side * half_cols, (side + 1) * half_cols)
+        z_copies[0, side].wait_recv()
+        z_copies[1, side].wait_recv()
+        grad = g_own[3, side] + g_z[0, side] + g_z[1, side]
+        inv = inv_ref[p, :, columns]
+        dirs = w_all[p, :, columns].astype(F32) * inv
+        col = jnp.sum(dirs * grad, axis=0, keepdims=True)
+        g_own[3, side] = (grad - dirs * col) * inv
+        to_all("dp", d, nd, lambda j, axis: remote(
+            g_own.at[3, side, pl.ds(j * own_depth, own_depth)], out_recv.at[side, d],
+            OUT_A2A + side, **{axis: j}))
+        out_recv[side, d] = g_own[3, side, own_rows]
+
     wait_bytes(rsem.at[LOSS_DP], loss_d.at[pl.ds(0, nd - 1)])
     whole = loss_d[0]
     for j in range(1, nd):
@@ -387,9 +411,11 @@
     loss_out[...] = jnp.broadcast_to(
         jnp.sum(jnp.sum(whole, axis=0, keepdims=True), axis=1, keepdims=True) * (1.0 / total_rows), (8, LANES))
 
-    wait_bytes(rsem.at[OUT_A2A], out_recv.at[pl.ds(0, nd - 1)])
-    for j in range(nd):
-        out[:, j * cols:(j + 1) * cols] = out_recv[j]
+    for side in (0, 1):
+        wait_bytes(rsem.at[OUT_A2A + side], out_recv.at[side, pl.ds(0, nd - 1)])
+        for j in range(nd):
+            base = j * cols + side * half_cols
+            out[:, base:base + half_cols] = out_recv[side, j]
 
     for copy in copies:
         copy.wait_send()
@@ -402,7 +428,8 @@
             wait_bytes(ssem.at[ROW[it]], rowx.at[it, pl.ds(0, nd - 1), 0])
         else:
             wait_bytes(ssem.at[ROW[it]], rowx.at[it, pl.ds(0, nd - 1)])
-    wait_bytes(ssem.at[OUT_A2A], out_recv.at[pl.ds(0, nd - 1)])
+    for side in (0, 1):
+        wait_bytes(ssem.at[OUT_A2A + side], out_recv.at[side, pl.ds(0, nd - 1)])
     wait_bytes(ssem.at[LOSS_PROTO], loss_p.at[pl.ds(0, np_ - 1)])
     wait_bytes(ssem.at[LOSS_DP], loss_d.at[pl.ds(0, nd - 1)])
 
@@ -440,14 +467,14 @@
             vmem((rows, LANES), F32),
             vmem((ITERS, np_, np_, 1, cols), F32),
             vmem((ITERS, nd, 2, rows // LANES, LANES), F32),
-            vmem((rows, cols), BF16),
-            vmem((4, depth, cols), F32),
-            vmem((4, depth, cols), F32),
-            vmem((4, depth, cols), F32),
-            vmem((depth // 2, cols), F32),
-            vmem((depth // 2, cols), F32),
-            vmem((2, depth, cols), F32),
-            vmem((nd, own_depth, cols), F32),
+            vmem((2, rows, cols // 2), BF16),
+            vmem((4, 2, depth, cols // 2), F32),
+            vmem((4, 2, depth, cols // 2), F32),
+            vmem((4, 2, depth, cols // 2), F32),
+            vmem((depth, cols // 2), F32),
+            vmem((depth, cols // 2), F32),
+            vmem((2, 2, depth, cols // 2), F32),
+            vmem((2, nd, own_depth, cols // 2), F32),
             vmem((np_, 8, LANES), F32),
             vmem((nd, 8, LANES), F32),
             pltpu.SemaphoreType.DMA((STAGES,)),

time: 147 us -> 124 us (0.84)
  Pallas kernels: 143 us -> 120 us
    pallas_call x1, Pallas kernels: 143 us -> 120 us  [body(): pl.pallas_call(functools.partial(kernel, nd, np_, tile), out_shape=(jax.S...]
where the time goes in v2:
time: 124 us; the launch traced here: 123 us
  Pallas kernels  120 us (97%)
  local copies, waits for them, and re-layouts  3.05 us (2%)
    pallas_call x1, Pallas kernels, body(): pl.pallas_call(functools.partial(kernel, nd, np_, tile), out_shape=(jax.S...  120 us

profile of v2, /device:TPU:0, one launch (start us, length us, event | category | flops | bytes accessed | tf_op | source)
XLA Modules:
  0.0 123.2 jit_solution(5773292189438632384)
XLA Ops:
  0.6 119.6 %shard_map.50 = (f32[16,8192]{1,0:T(8,128)}, f32[8,128]{1,0:T(8,128)}) custom-call(bf16[1024,256]{1,0:T(8,128)(2,1)} %teacher.1, bf16[1024,256]{1,0:T(8,128)(2,1)} %student.1, bf16[16,8192]{1,0:T(8,128)(2,1)} %weight.1), custom_call_target="tpu_custom_call" | custom-call | flops 12884901888 | bytes 2097152 | tf_op jit(solution)/shard_map/pallas_call | solution.py:444
  120.2 1.2 slice.3
  121.4 1.9 %copy.6 = f32[16,8192]{1,0:T(8,128)} copy(f32[16,8192]{1,0:T(8,128)} %get-tuple-element.8) | data formatting | bytes 1048576

commit v3 on v2

--- a/solution.py
+++ b/solution.py
@@ -19,16 +19,18 @@
 BF16 = jnp.bfloat16
 
 W_A2A, T_GATHER, S_GATHER = 0, 1, 2
-COL = (3, 4, 5)
-ROW = (6, 7, 8)
-LOSS_PROTO, LOSS_DP = 10, 11
-W_PLUS, W_MINUS, W_HALF_A, W_HALF_B = 12, 13, 14, 15
+SOFT = 3
+LOSS_PROTO, LOSS_DP = 4, 5
+W_PLUS, W_MINUS = 6, 8
+W_HALF_A, W_HALF_B = 10, 11
 W_CORE = 16
 G_CORE = 20
 G_HALF_A, G_HALF_B = 28, 29
 G_PLUS, G_MINUS = 30, 32
 OUT_A2A = 34
-STAGES = 36
+COL = 36
+ROW = 42
+STAGES = 48
 
 
 def unit_rows(feat):
@@ -55,7 +57,7 @@
     out, loss_out,
     t_raw, s_raw, t_all, s_all, s_t, w_all, e_ref,
     at_ref, as_ref, inv_ref, v_ref, rb_ref, sb_ref, racc, sacc,
-    colx, rowx, g_tiles, g_send, g_recv, g_own, half_a, half_b, g_z, out_recv,
+    cacc, colx, rowx, soft, g_tiles, g_send, g_recv, g_own, half_a, half_b, g_z, out_recv,
     loss_p, loss_d,
     ssem, rsem, lsem,
 ):
@@ -131,17 +133,26 @@
         return copy
 
     opposite = lax.rem(p + 4, np_)
-    up = go(remote(w_all.at[p], w_all.at[p], W_PLUS, proto=plus))
-    down = go(remote(w_all.at[p], w_all.at[p], W_MINUS, proto=minus))
+    def ring(part, stage, to):
+        return remote(w_all.at[p, part], w_all.at[p, part], stage, proto=to)
+
+    up_top = go(ring(top, W_PLUS, plus))
+    down_bottom = go(ring(bottom, W_MINUS, minus))
     core = [None] * 4
     core[0] = go(remote(w_all.at[p], w_all.at[p], W_CORE, proto=partner))
     to_all("dp", d, nd, lambda j, axis: remote(
         t_all.at[own_chunk], t_all.at[own_chunk], T_GATHER, **{axis: j}))
-    up.wait_recv()
+    up_top.wait_send()
+    up_bottom = go(ring(bottom, W_PLUS + 1, plus))
+    down_bottom.wait_send()
+    down_top = go(ring(top, W_MINUS + 1, minus))
+    up_top.wait_recv()
     pass_a = go(remote(w_all.at[minus, top], w_all.at[minus, top], W_HALF_A, proto=plus))
+    down_bottom.wait_recv()
+    pass_b = go(remote(w_all.at[plus, bottom], w_all.at[plus, bottom], W_HALF_B, proto=minus))
+    up_bottom.wait_recv()
     core[1] = go(remote(w_all.at[minus], w_all.at[minus], W_CORE + 1, proto=partner))
-    down.wait_recv()
-    pass_b = go(remote(w_all.at[plus, bottom], w_all.at[plus, bottom], W_HALF_B, proto=minus))
+    down_top.wait_recv()
     core[2] = go(remote(w_all.at[plus], w_all.at[plus], W_CORE + 2, proto=partner))
 
     wait_bytes(rsem.at[T_GATHER], t_all.at[pl.ds(0, rows - chunk)])
@@ -180,56 +191,60 @@
     core[3].wait_recv()
     first_pass(other(opposite))
 
-    def send_cols(it):
-        to_all("proto", p, np_, lambda j, axis: remote(
-            colx.at[it, p], colx.at[it, p], COL[it], **{axis: j}))
-
-    def take_cols(it):
-        wait_bytes(rsem.at[COL[it]], colx.at[it, pl.ds(0, np_ - 1)])
-        mass = colx[it, 0]
+    half_blocks, half_rows = np_ // 2, rows // 2
+    lines = rows // LANES
+    half_lines = lines // 2
+    lane_chunks = cols // LANES
+
+    def some_blocks(h):
+        return pl.ds(h * half_blocks, half_blocks)
+
+    def some_lines(h):
+        return pl.ds(h * half_lines, half_lines)
+
+    def send_cols(it, h):
+        mine = colx.at[it, p, some_blocks(h)]
+        to_all("proto", p, np_, lambda j, axis: remote(mine, mine, COL + 2 * it + h, **{axis: j}))
+
+    def take_cols(it, h):
+        wait_bytes(rsem.at[COL + 2 * it + h], colx.at[it, pl.ds(0, np_ - 1), some_blocks(h)])
+        mass = colx[it, 0, some_blocks(h)]
         for j in range(1, np_):
-            mass = mass + colx[it, j]
-        v_ref[...] = 1.0 / (mass * total_cols)
-
-    def dense(acc_ref):
-        lines = [
+            mass = mass + colx[it, j, some_blocks(h)]
+        v_ref[some_blocks(h)] = 1.0 / (mass * total_cols)
+
+    def dense(acc_ref, first, last):
+        sums = [
             jnp.sum(acc_ref[c * LANES:(c + 1) * LANES, :].T, axis=0, keepdims=True)
-            for c in range(rows // LANES)]
-        return jnp.concatenate(lines, axis=0)
-
-    def spread(x, ref):
-        for c in range(rows // LANES):
-            ref[c * LANES:(c + 1) * LANES, :] = jnp.broadcast_to(x[c:c + 1, :], (LANES, LANES)).T
-
-    def send_rows(it):
-        def make(j, axis):
-            if it < ITERS - 1:
-                return remote(rowx.at[it, d, 0], rowx.at[it, d, 0], ROW[it], **{axis: j})
-            return remote(rowx.at[it, d], rowx.at[it, d], ROW[it], **{axis: j})
-        to_all("dp", d, nd, make)
-
-    def row_total(it, kind):
-        total = rowx[it, 0, kind]
+            for c in range(first, last)]
+        return jnp.concatenate(sums, axis=0)
+
+    def spread(x, ref, first):
+        for c in range(x.shape[0]):
+            at = (first + c) * LANES
+            ref[at:at + LANES, :] = jnp.broadcast_to(x[c:c + 1, :], (LANES, LANES)).T
+
+    def send_rows(it, h):
+        mine = rowx.at[it, d, some_lines(h)]
+        to_all("dp", d, nd, lambda j, axis: remote(mine, mine, ROW + 2 * it + h, **{axis: j}))
+
+    def row_total(it, first, last):
+        total = rowx[it, 0, first:last]
         for j in range(1, nd):
-            total = total + rowx[it, j, kind]
+            total = total + rowx[it, j, first:last]
         return total
 
-    def take_rows(it):
-        if it < ITERS - 1:
-            wait_bytes(rsem.at[ROW[it]], rowx.at[it, pl.ds(0, nd - 1), 0])
-        else:
-            wait_bytes(rsem.at[ROW[it]], rowx.at[it, pl.ds(0, nd - 1)])
-        return 1.0 / (row_total(it, 0) * total_rows)
-
-    lane_chunks = cols // LANES
-
-    def row_pass(it):
+    def take_rows(it, h):
+        wait_bytes(rsem.at[ROW + 2 * it + h], rowx.at[it, pl.ds(0, nd - 1), some_lines(h)])
+        return 1.0 / (row_total(it, h * half_lines, (h + 1) * half_lines) * total_rows)
+
+    def row_part(hb, hr):
         span = 64
 
         def step(i, carry):
-            part = pl.ds(i * span, span)
-            acc = None
-            for b in range(np_):
+            part = pl.ds(hr * half_rows + i * span, span)
+            acc = None if hb == 0 else racc[part, :]
+            for b in range(hb * half_blocks, (hb + 1) * half_blocks):
                 for j in range(lane_chunks):
                     lanes = slice(j * LANES, (j + 1) * LANES)
                     term = e_ref[b, part, lanes] * v_ref[b, :, lanes]
@@ -237,17 +252,27 @@
             racc[part, :] = acc
             return carry
 
-        lax.fori_loop(0, rows // span, step, 0)
-        rowx[it, d, 0] = dense(racc)
-
-    def col_pass(it):
+        lax.fori_loop(0, half_rows // span, step, 0, unroll=True)
+
+    def row_pass(it):
+        take_cols(it, 0)
+        row_part(0, 0)
+        row_part(0, 1)
+        take_cols(it, 1)
+        for h in range(2):
+            row_part(1, h)
+            first, last = h * half_lines, (h + 1) * half_lines
+            rowx[it, d, first:last] = dense(racc, first, last)
+            send_rows(it, h)
+
+    def col_part(it, hr, first, last):
         pair = 2
 
         def step(b2, carry):
             def inner(i, accs):
                 accs = list(accs)
                 for g in range(8):
-                    part = pl.ds(i * 64 + g * 8, 8)
+                    part = pl.ds(hr * half_rows + i * 64 + g * 8, 8)
                     r = rb_ref[part, :]
                     for k in range(pair):
                         for j in range(lane_chunks):
@@ -255,15 +280,29 @@
                             accs[n] = accs[n] + e_ref[b2 * pair + k, part, j * LANES:(j + 1) * LANES] * r
                 return tuple(accs)
 
-            zero = jnp.zeros((8, LANES), F32)
-            accs = lax.fori_loop(0, rows // 64, inner, (zero,) * (pair * lane_chunks))
-            for k in range(pair):
-                for j in range(lane_chunks):
-                    colx[it, p, b2 * pair + k, :, j * LANES:(j + 1) * LANES] = jnp.sum(
-                        accs[k * lane_chunks + j], axis=0, keepdims=True)
+            spots = [(b2 * pair + k, slice(j * LANES, (j + 1) * LANES))
+                     for k in range(pair) for j in range(lane_chunks)]
+            if hr == 0:
+                init = (jnp.zeros((8, LANES), F32),) * len(spots)
+            else:
+                init = tuple(cacc[b, :, lanes] for b, lanes in spots)
+            accs = lax.fori_loop(0, half_rows // 64, inner, init, unroll=min(4, half_rows // 64))
+            for acc, (b, lanes) in zip(accs, spots):
+                if hr == 0:
+                    cacc[b, :, lanes] = acc
+                else:
+                    colx[it, p, b, :, lanes] = jnp.sum(acc, axis=0, keepdims=True)
             return carry
 
-        lax.fori_loop(0, np_ // pair, step, 0)
+        lax.fori_loop(first // pair, last // pair, step, 0)
+
+    def col_pass(it):
+        spread(take_rows(it - 1, 0), rb_ref, 0)
+        col_part(it, 0, 0, np_)
+        spread(take_rows(it - 1, 1), rb_ref, half_lines)
+        for h in range(2):
+            col_part(it, 1, h * half_blocks, (h + 1) * half_blocks)
+            send_cols(it, h)
 
     def student_pass(first, last):
         def step(block, carry):
@@ -275,36 +314,30 @@
             return carry
         lax.fori_loop(first, last, step, 0)
 
-    send_cols(0)
+    send_cols(0, 0)
+    send_cols(0, 1)
+    sacc[...] = jnp.zeros_like(sacc)
+    row_pass(0)
     wait_bytes(rsem.at[S_GATHER], s_all.at[pl.ds(0, rows - chunk)])
-    for c in range(rows // LANES):
+    for c in range(lines):
         s_t[:, c * LANES:(c + 1) * LANES] = s_all[c * LANES:(c + 1) * LANES, :].T
-    sacc[...] = jnp.zeros_like(sacc)
-    student_pass(0, 2)
-    take_cols(0)
-    row_pass(0)
-    send_rows(0)
-    student_pass(2, 4)
-    spread(take_rows(0), rb_ref)
+    student_pass(0, 4)
     col_pass(1)
-    send_cols(1)
     student_pass(4, 6)
-    take_cols(1)
     row_pass(1)
-    send_rows(1)
     student_pass(6, 8)
-    rowx[2, d, 1] = dense(sacc)
-    spread(take_rows(1), rb_ref)
+    soft[d] = dense(sacc, 0, lines)
+    to_all("dp", d, nd, lambda j, axis: remote(soft.at[d], soft.at[d], SOFT, **{axis: j}))
     col_pass(2)
-    send_cols(2)
-    take_cols(2)
+    wait_bytes(rsem.at[SOFT], soft.at[pl.ds(0, nd - 1)])
+    soft_total = soft[0]
+    for j in range(1, nd):
+        soft_total = soft_total + soft[j]
+    spread(1.0 / (soft_total * (total_rows * STUDENT_TEMP)), sb_ref, 0)
+    lse = jnp.log(soft_total)
     row_pass(2)
-    send_rows(2)
-    row_scale = take_rows(2)
-    spread(row_scale * (1.0 / STUDENT_TEMP), rb_ref)
-    soft_total = row_total(2, 1)
-    spread(1.0 / (soft_total * (total_rows * STUDENT_TEMP)), sb_ref)
-    lse = jnp.log(soft_total)
+    for h in range(2):
+        spread(take_rows(2, h) * (1.0 / STUDENT_TEMP), rb_ref, h * half_lines)
 
     half_cols = cols // 2
 
@@ -408,8 +441,7 @@
     whole = loss_d[0]
     for j in range(1, nd):
         whole = whole + loss_d[j]
-    loss_out[...] = jnp.broadcast_to(
-        jnp.sum(jnp.sum(whole, axis=0, keepdims=True), axis=1, keepdims=True) * (1.0 / total_rows), (8, LANES))
+    loss_out[0, 0] = jnp.sum(whole) * (1.0 / total_rows)
 
     for side in (0, 1):
         wait_bytes(rsem.at[OUT_A2A + side], out_recv.at[side, pl.ds(0, nd - 1)])
@@ -418,16 +450,16 @@
             out[:, base:base + half_cols] = out_recv[side, j]
 
     for copy in copies:
-        copy.wait_send()
+        if copy is not up_top and copy is not down_bottom:
+            copy.wait_send()
     wait_bytes(ssem.at[W_A2A], w_all.at[0, pl.ds(0, depth - own_depth)])
     wait_bytes(ssem.at[T_GATHER], t_all.at[pl.ds(0, rows - chunk)])
     wait_bytes(ssem.at[S_GATHER], s_all.at[pl.ds(0, rows - chunk)])
     for it in range(ITERS):
-        wait_bytes(ssem.at[COL[it]], colx.at[it, pl.ds(0, np_ - 1)])
-        if it < ITERS - 1:
-            wait_bytes(ssem.at[ROW[it]], rowx.at[it, pl.ds(0, nd - 1), 0])
-        else:
-            wait_bytes(ssem.at[ROW[it]], rowx.at[it, pl.ds(0, nd - 1)])
+        for h in range(2):
+            wait_bytes(ssem.at[COL + 2 * it + h], colx.at[it, pl.ds(0, np_ - 1), some_blocks(h)])
+            wait_bytes(ssem.at[ROW + 2 * it + h], rowx.at[it, pl.ds(0, nd - 1), some_lines(h)])
+    wait_bytes(ssem.at[SOFT], soft.at[pl.ds(0, nd - 1)])
     for side in (0, 1):
         wait_bytes(ssem.at[OUT_A2A + side], out_recv.at[side, pl.ds(0, nd - 1)])
     wait_bytes(ssem.at[LOSS_PROTO], loss_p.at[pl.ds(0, np_ - 1)])
@@ -445,10 +477,10 @@
         functools.partial(kernel, nd, np_, tile),
         out_shape=(
             jax.ShapeDtypeStruct((own_depth, block_cols), F32),
-            jax.ShapeDtypeStruct((8, LANES), F32),
+            jax.ShapeDtypeStruct((1, 1), F32),
         ),
         in_specs=[pl.BlockSpec(memory_space=pl.ANY)] * 3,
-        out_specs=[pl.BlockSpec(memory_space=vmem)] * 2,
+        out_specs=[pl.BlockSpec(memory_space=vmem), pl.BlockSpec(memory_space=pltpu.SMEM)],
         scratch_shapes=[
             vmem((chunk, depth), BF16),
             vmem((chunk, depth), BF16),
@@ -465,8 +497,10 @@
             vmem((rows, LANES), F32),
             vmem((rows, LANES), F32),
             vmem((rows, LANES), F32),
+            vmem((np_, 8, cols), F32),
             vmem((ITERS, np_, np_, 1, cols), F32),
-            vmem((ITERS, nd, 2, rows // LANES, LANES), F32),
+            vmem((ITERS, nd, rows // LANES, LANES), F32),
+            vmem((nd, rows // LANES, LANES), F32),
             vmem((2, rows, cols // 2), BF16),
             vmem((4, 2, depth, cols // 2), F32),
             vmem((4, 2, depth, cols // 2), F32),
@@ -487,7 +521,7 @@
             flops=6 * rows * cols * np_ * depth, bytes_accessed=2 ** 21,
             transcendentals=2 * rows * cols * np_),
     )(teacher_feat, student_feat, proto_weight)
-    return out, loss[0, 0]
+    return out, jnp.reshape(loss, ())
 
 
 def solution(mesh):

time: 124 us -> 111 us (0.90)
  Pallas kernels: 120 us -> 107 us
  between operations: 0.64 us -> 2.34 us
    pallas_call x1, Pallas kernels: 120 us -> 107 us  [body(): pl.pallas_call(functools.partial(kernel, nd, np_, tile), out_shape=(jax.S...]
where the time goes in v3:
time: 111 us
  Pallas kernels  107 us (96%)
  between operations  2.34 us (2%)
  local copies, waits for them, and re-layouts  1.87 us (2%)
    pallas_call x1, Pallas kernels, body(): pl.pallas_call(functools.partial(kernel, nd, np_, tile), out_shape=(jax.S...  107 us

profile of v3, /device:TPU:0, one launch (start us, length us, event | category | flops | bytes accessed | tf_op | source)
XLA Modules:
  0.0 110.7 jit_solution(11395256756973398167)
XLA Ops:
  0.6 106.5 %shard_map.50 = (f32[16,8192]{1,0:T(8,128)}, f32[1,1]{1,0:T(1,128)}) custom-call(bf16[1024,256]{1,0:T(8,128)(2,1)} %teacher.1, bf16[1024,256]{1,0:T(8,128)(2,1)} %student.1, bf16[16,8192]{1,0:T(8,128)(2,1)} %weight.1), custom_call_target="tpu_custom_call" | custom-call | flops 12884901888 | bytes 2097152 | tf_op jit(solution)/shard_map/pallas_call | solution.py:476
  107.2 1.9 %copy.7 = f32[16,8192]{1,0:T(8,128)} copy(f32[16,8192]{1,0:T(8,128)} %get-tuple-element.8) | data formatting | bytes 1048576

commit v4 on v3

--- a/solution.py
+++ b/solution.py
@@ -26,11 +26,12 @@
 W_CORE = 16
 G_CORE = 20
 G_HALF_A, G_HALF_B = 28, 29
-G_PLUS, G_MINUS = 30, 32
-OUT_A2A = 34
+G_PLUS, G_MINUS = 30, 31
+G_LAST = 32
+OUT_A2A = 48
 COL = 36
 ROW = 42
-STAGES = 48
+STAGES = 52
 
 
 def unit_rows(feat):
@@ -57,7 +58,7 @@
     out, loss_out,
     t_raw, s_raw, t_all, s_all, s_t, w_all, e_ref,
     at_ref, as_ref, inv_ref, v_ref, rb_ref, sb_ref, racc, sacc,
-    cacc, colx, rowx, soft, g_tiles, g_send, g_recv, g_own, half_a, half_b, g_z, out_recv,
+    cacc, colx, rowx, soft, g_tiles, g_send, g_recv, g_own, half_a, half_b, g_z, out_send, out_recv,
     loss_p, loss_d,
     ssem, rsem, lsem,
 ):
@@ -142,9 +143,7 @@
     core[0] = go(remote(w_all.at[p], w_all.at[p], W_CORE, proto=partner))
     to_all("dp", d, nd, lambda j, axis: remote(
         t_all.at[own_chunk], t_all.at[own_chunk], T_GATHER, **{axis: j}))
-    up_top.wait_send()
     up_bottom = go(ring(bottom, W_PLUS + 1, plus))
-    down_bottom.wait_send()
     down_top = go(ring(top, W_MINUS + 1, minus))
     up_top.wait_recv()
     pass_a = go(remote(w_all.at[minus, top], w_all.at[minus, top], W_HALF_A, proto=plus))
@@ -339,7 +338,7 @@
     for h in range(2):
         spread(take_rows(2, h) * (1.0 / STUDENT_TEMP), rb_ref, h * half_lines)
 
-    half_cols = cols // 2
+    half_cols, quarter_cols = cols // 2, cols // 4
 
     def unit(block, side, g_tile, acc):
         base = side * half_cols
@@ -378,80 +377,103 @@
             z_copies["a"] = go(remote(mine, half_a, G_HALF_A, proto=plus))
         elif (n, side) == (0, 1):
             z_copies["b"] = go(remote(mine, half_b, G_HALF_B, proto=minus))
-        elif n == 1:
-            z_copies[0, side] = go(remote(mine, g_z.at[0, side], G_PLUS + side, proto=plus))
-        elif n == 2:
-            z_copies[1, side] = go(remote(mine, g_z.at[1, side], G_MINUS + side, proto=minus))
+        elif (n, side) == (1, 1):
+            z_copies["plus"] = go(remote(mine, g_z.at[0, 1], G_PLUS, proto=plus))
+        elif (n, side) == (2, 0):
+            z_copies["minus"] = go(remote(mine, g_z.at[1, 0], G_MINUS, proto=minus))
+        elif n != 3:
+            send_last(side, 0)
+
+    def send_last(side, quarter):
+        lanes = pl.ds(quarter * quarter_cols, quarter_cols)
+        to = plus if side == 0 else minus
+        z_copies[side, quarter] = go(remote(
+            g_own.at[side + 1, side, :, lanes], g_z.at[side, side, :, lanes],
+            G_LAST + 2 * quarter + side, proto=to))
 
     def gradient(n, side, is_own, g_tile):
         dst = g_own if is_own else g_send
         dst[n, side] = jnp.dot(s_t[...], g_tile[...], preferred_element_type=F32)
+
+    def send_core(n, side):
+        core_copies[n, side] = go(remote(
+            g_send.at[n, side], g_recv.at[n, side], G_CORE + 2 * n + side, proto=partner))
 
     order = [(0, 0), (0, 1), (1, 1), (2, 0), (3, 0), (3, 1), (1, 0), (2, 1)]
     units = [(n, side, is_own) for n, side in order for is_own in (False, True)]
     loss_acc = jnp.zeros((8, LANES), F32)
     waiting = None
     for k in range(len(units) + 2):
-        if 0 < k <= len(units):
+        if 2 < k <= len(units):
             gradient(*units[k - 1], g_tiles.at[(k - 1) % 2])
         if k < len(units):
             n, side, is_own = units[k]
             block = owners[n] if is_own else other(owners[n])
             loss_acc = unit(block, side, g_tiles.at[k % 2], loss_acc)
+        if k < 2:
+            gradient(*units[k], g_tiles.at[k % 2])
+        if k == 0:
+            send_core(*units[0][:2])
+        elif k == 1:
+            chip_sum(*units[1][:2])
         if waiting is not None:
             chip_sum(*waiting)
             waiting = None
-        if 0 < k <= len(units):
-            n, side, is_own = units[k - 1]
-            if is_own:
-                waiting = (n, side)
+        if 2 < k <= len(units):
+            if units[k - 1][2]:
+                waiting = units[k - 1][:2]
             else:
-                core_copies[n, side] = go(remote(
-                    g_send.at[n, side], g_recv.at[n, side], G_CORE + 2 * n + side, proto=partner))
+                send_core(*units[k - 1][:2])
+    first_quarters = [z_copies[0, 0], z_copies[1, 0]]
+    for side in (0, 1):
+        send_last(side, 1)
 
     first_line = lax.broadcasted_iota(jnp.int32, (8, LANES), 0) == 0
     lse_sum = jnp.broadcast_to(jnp.sum(lse, axis=0, keepdims=True) * (1.0 / nd), (8, LANES))
     loss_scale = total_rows * STUDENT_TEMP / LOG2E
-    loss_p[p] = jnp.where(first_line, lse_sum, 0.0) - loss_acc * loss_scale
+    loss_d[d] = jnp.where(first_line, lse_sum, 0.0) - loss_acc * loss_scale
+    to_all("dp", d, nd, lambda j, axis: remote(
+        loss_d.at[d], loss_d.at[d], LOSS_DP, **{axis: j}))
+    wait_bytes(rsem.at[LOSS_DP], loss_d.at[pl.ds(0, nd - 1)])
+    part = loss_d[0]
+    for j in range(1, nd):
+        part = part + loss_d[j]
+    loss_p[p] = part
     to_all("proto", p, np_, lambda j, axis: remote(
         loss_p.at[p], loss_p.at[p], LOSS_PROTO, **{axis: j}))
+
+    for quarter in (0, 1):
+        lanes = slice(quarter * quarter_cols, (quarter + 1) * quarter_cols)
+        for side in (0, 1):
+            if quarter == 0:
+                z_copies["minus" if side == 0 else "plus"].wait_recv()
+            z_copies[side, quarter].wait_recv()
+            n = 2 * quarter + side
+            columns = slice(side * half_cols + lanes.start, side * half_cols + lanes.stop)
+            grad = g_own[3, side, :, lanes] + g_z[0, side, :, lanes] + g_z[1, side, :, lanes]
+            inv = inv_ref[p, :, columns]
+            dirs = w_all[p, :, columns].astype(F32) * inv
+            col = jnp.sum(dirs * grad, axis=0, keepdims=True)
+            out_send[n] = (grad - dirs * col) * inv
+            to_all("dp", d, nd, lambda j, axis: remote(
+                out_send.at[n, pl.ds(j * own_depth, own_depth)], out_recv.at[n, d],
+                OUT_A2A + n, **{axis: j}))
+            out_recv[n, d] = out_send[n, own_rows]
+
+    for n in range(4):
+        wait_bytes(rsem.at[OUT_A2A + n], out_recv.at[n, pl.ds(0, nd - 1)])
+        for j in range(nd):
+            base = j * cols + (n % 2) * half_cols + (n // 2) * quarter_cols
+            out[:, base:base + quarter_cols] = out_recv[n, j]
+
     wait_bytes(rsem.at[LOSS_PROTO], loss_p.at[pl.ds(0, np_ - 1)])
-    part = loss_p[0]
+    whole = loss_p[0]
     for j in range(1, np_):
-        part = part + loss_p[j]
-    loss_d[d] = part
-    to_all("dp", d, nd, lambda j, axis: remote(
-        loss_d.at[d], loss_d.at[d], LOSS_DP, **{axis: j}))
-
-    for side in (0, 1):
-        columns = slice(side * half_cols, (side + 1) * half_cols)
-        z_copies[0, side].wait_recv()
-        z_copies[1, side].wait_recv()
-        grad = g_own[3, side] + g_z[0, side] + g_z[1, side]
-        inv = inv_ref[p, :, columns]
-        dirs = w_all[p, :, columns].astype(F32) * inv
-        col = jnp.sum(dirs * grad, axis=0, keepdims=True)
-        g_own[3, side] = (grad - dirs * col) * inv
-        to_all("dp", d, nd, lambda j, axis: remote(
-            g_own.at[3, side, pl.ds(j * own_depth, own_depth)], out_recv.at[side, d],
-            OUT_A2A + side, **{axis: j}))
-        out_recv[side, d] = g_own[3, side, own_rows]
-
-    wait_bytes(rsem.at[LOSS_DP], loss_d.at[pl.ds(0, nd - 1)])
-    whole = loss_d[0]
-    for j in range(1, nd):
-        whole = whole + loss_d[j]
+        whole = whole + loss_p[j]
     loss_out[0, 0] = jnp.sum(whole) * (1.0 / total_rows)
 
-    for side in (0, 1):
-        wait_bytes(rsem.at[OUT_A2A + side], out_recv.at[side, pl.ds(0, nd - 1)])
-        for j in range(nd):
-            base = j * cols + side * half_cols
-            out[:, base:base + half_cols] = out_recv[side, j]
-
     for copy in copies:
-        if copy is not up_top and copy is not down_bottom:
-            copy.wait_send()
+        copy.wait_send()
     wait_bytes(ssem.at[W_A2A], w_all.at[0, pl.ds(0, depth - own_depth)])
     wait_bytes(ssem.at[T_GATHER], t_all.at[pl.ds(0, rows - chunk)])
     wait_bytes(ssem.at[S_GATHER], s_all.at[pl.ds(0, rows - chunk)])
@@ -460,8 +482,8 @@
             wait_bytes(ssem.at[COL + 2 * it + h], colx.at[it, pl.ds(0, np_ - 1), some_blocks(h)])
             wait_bytes(ssem.at[ROW + 2 * it + h], rowx.at[it, pl.ds(0, nd - 1), some_lines(h)])
     wait_bytes(ssem.at[SOFT], soft.at[pl.ds(0, nd - 1)])
-    for side in (0, 1):
-        wait_bytes(ssem.at[OUT_A2A + side], out_recv.at[side, pl.ds(0, nd - 1)])
+    for n in range(4):
+        wait_bytes(ssem.at[OUT_A2A + n], out_recv.at[n, pl.ds(0, nd - 1)])
     wait_bytes(ssem.at[LOSS_PROTO], loss_p.at[pl.ds(0, np_ - 1)])
     wait_bytes(ssem.at[LOSS_DP], loss_d.at[pl.ds(0, nd - 1)])
 
@@ -508,7 +530,8 @@
             vmem((depth, cols // 2), F32),
             vmem((depth, cols // 2), F32),
             vmem((2, 2, depth, cols // 2), F32),
-            vmem((2, nd, own_depth, cols // 2), F32),
+            vmem((4, depth, cols // 4), F32),
+            vmem((4, nd, own_depth, cols // 4), F32),
             vmem((np_, 8, LANES), F32),
             vmem((nd, 8, LANES), F32),
             pltpu.SemaphoreType.DMA((STAGES,)),

time: 111 us -> 108 us (0.973)
  Pallas kernels: 107 us -> 103 us
    pallas_call x1, Pallas kernels: 107 us -> 103 us  [body(): pl.pallas_call(functools.partial(kernel, nd, np_, tile), out_shape=(jax.S...]
where the time goes in v4:
time: 108 us; the launch traced here: 107 us
  Pallas kernels  103 us (95%)
  between operations  2.34 us (2%)
  local copies, waits for them, and re-layouts  1.87 us (2%)
    pallas_call x1, Pallas kernels, body(): pl.pallas_call(functools.partial(kernel, nd, np_, tile), out_shape=(jax.S...  103 us

profile of v4, /device:TPU:0, one launch (start us, length us, event | category | flops | bytes accessed | tf_op | source)
XLA Modules:
  0.0 107.3 jit_solution(8643243652199614978)
XLA Ops:
  0.6 103.1 %shard_map.50 = (f32[16,8192]{1,0:T(8,128)}, f32[1,1]{1,0:T(1,128)}) custom-call(bf16[1024,256]{1,0:T(8,128)(2,1)} %teacher.1, bf16[1024,256]{1,0:T(8,128)(2,1)} %student.1, bf16[16,8192]{1,0:T(8,128)(2,1)} %weight.1), custom_call_target="tpu_custom_call" | custom-call | flops 12884901888 | bytes 2097152 | tf_op jit(solution)/shard_map/pallas_call | solution.py:498
  103.7 1.9 %copy.7 = f32[16,8192]{1,0:T(8,128)} copy(f32[16,8192]{1,0:T(8,128)} %get-tuple-element.8) | data formatting | bytes 1048576

commit v5 on v4

--- a/solution.py
+++ b/solution.py
@@ -56,7 +56,7 @@
     nd, np_, tile,
     teacher, student, weight,
     out, loss_out,
-    t_raw, s_raw, t_all, s_all, s_t, w_all, e_ref,
+    t_raw, s_raw, w_raw, t_all, s_all, s_t, w_all, e_ref,
     at_ref, as_ref, inv_ref, v_ref, rb_ref, sb_ref, racc, sacc,
     cacc, colx, rowx, soft, g_tiles, g_send, g_recv, g_own, half_a, half_b, g_z, out_send, out_recv,
     loss_p, loss_d,
@@ -108,17 +108,20 @@
     load_s = pltpu.make_async_copy(student.at[pl.ds(p * chunk, chunk)], s_raw, lsem.at[1])
     own_rows = pl.ds(d * own_depth, own_depth)
     load_w = pltpu.make_async_copy(
-        weight.at[:, pl.ds(d * cols, cols)], w_all.at[p, own_rows], lsem.at[2])
+        w_raw.at[:, pl.ds(d * cols, cols)], w_all.at[p, own_rows], lsem.at[2])
+    load_raw = pltpu.make_async_copy(weight, w_raw, lsem.at[3])
     load_t.start()
+    load_raw.start()
     load_s.start()
-    load_w.start()
     load_t.wait()
     own_chunk = pl.ds(d * chunk, chunk)
     t_all[own_chunk, :] = unit_rows(t_raw[...])
+    load_raw.wait()
+    load_w.start()
     pl.semaphore_wait(barrier, nd + np_ - 2)
 
     to_all("dp", d, nd, lambda j, axis: remote(
-        weight.at[:, pl.ds(j * cols, cols)], w_all.at[p, own_rows], W_A2A, **{axis: j}))
+        w_raw.at[:, pl.ds(j * cols, cols)], w_all.at[p, own_rows], W_A2A, **{axis: j}))
     load_s.wait()
     s_all[own_chunk, :] = unit_rows(s_raw[...])
 
@@ -285,7 +288,7 @@
                 init = (jnp.zeros((8, LANES), F32),) * len(spots)
             else:
                 init = tuple(cacc[b, :, lanes] for b, lanes in spots)
-            accs = lax.fori_loop(0, half_rows // 64, inner, init, unroll=min(4, half_rows // 64))
+            accs = lax.fori_loop(0, half_rows // 64, inner, init, unroll=min(8, half_rows // 64))
             for acc, (b, lanes) in zip(accs, spots):
                 if hr == 0:
                     cacc[b, :, lanes] = acc
@@ -317,14 +320,13 @@
     send_cols(0, 1)
     sacc[...] = jnp.zeros_like(sacc)
     row_pass(0)
+    col_pass(1)
     wait_bytes(rsem.at[S_GATHER], s_all.at[pl.ds(0, rows - chunk)])
     for c in range(lines):
         s_t[:, c * LANES:(c + 1) * LANES] = s_all[c * LANES:(c + 1) * LANES, :].T
     student_pass(0, 4)
-    col_pass(1)
-    student_pass(4, 6)
     row_pass(1)
-    student_pass(6, 8)
+    student_pass(4, 8)
     soft[d] = dense(sacc, 0, lines)
     to_all("dp", d, nd, lambda j, axis: remote(soft.at[d], soft.at[d], SOFT, **{axis: j}))
     col_pass(2)
@@ -506,6 +508,7 @@
         scratch_shapes=[
             vmem((chunk, depth), BF16),
             vmem((chunk, depth), BF16),
+            vmem((own_depth, block_cols), BF16),
             vmem((rows, depth), BF16),
             vmem((rows, depth), BF16),
             vmem((depth, rows), BF16),
@@ -536,7 +539,7 @@
             vmem((nd, 8, LANES), F32),
             pltpu.SemaphoreType.DMA((STAGES,)),
             pltpu.SemaphoreType.DMA((STAGES,)),
-            pltpu.SemaphoreType.DMA((3,)),
+            pltpu.SemaphoreType.DMA((4,)),
         ],
         compiler_params=pltpu.CompilerParams(
             collective_id=0, has_side_effects=True, vmem_limit_bytes=62 * 1024 * 1024),

time: 108 us -> 107 us (level)
  no operation moved by 1% of the time
where the time goes in v5:
time: 107 us
  Pallas kernels  103 us (96%)
  between operations  2.34 us (2%)
  local copies, waits for them, and re-layouts  1.87 us (2%)
    pallas_call x1, Pallas kernels, body(): pl.pallas_call(functools.partial(kernel, nd, np_, tile), out_shape=(jax.S...  103 us

profile of v5, /device:TPU:0, one launch (start us, length us, event | category | flops | bytes accessed | tf_op | source)
XLA Modules:
  0.0 106.8 jit_solution(8243703698709135522)
XLA Ops:
  0.6 102.6 %shard_map.50 = (f32[16,8192]{1,0:T(8,128)}, f32[1,1]{1,0:T(1,128)}) custom-call(bf16[1024,256]{1,0:T(8,128)(2,1)} %teacher.1, bf16[1024,256]{1,0:T(8,128)(2,1)} %student.1, bf16[16,8192]{1,0:T(8,128)(2,1)} %weight.1), custom_call_target="tpu_custom_call" | custom-call | flops 12884901888 | bytes 2097152 | tf_op jit(solution)/shard_map/pallas_call | solution.py:500
  103.2 1.9 %copy.7 = f32[16,8192]{1,0:T(8,128)} copy(f32[16,8192]{1,0:T(8,128)} %get-tuple-element.8) | data formatting | bytes 1048576
